TPU v7x, 32 devices: a whole 2x2x4 slice. The times are simulated.
32 devices in a mesh: tok: 8 (over z, x), head: 4 (over y, core).
Axes of the slice: x: 2, y: 2, z: 4, core: 2. Of those that a mesh axis runs over, the one named last changes fastest.
Arguments:
- head_inputs: bfloat16 [4096, 2048], P('tok', 'head'), may hold values from -6 to 6
- state_keys: bfloat16 [4096, 128], P('tok'), may hold values from -2 to 2
- state_queries: bfloat16 [4096, 128], P('tok'), may hold values from -2 to 2
- log_decay: float32 [4096, 32], P('tok', 'head'), may hold values from -1.6 to 0, as said below
- level_weight: float32 [4096, 32, 18], P('tok', 'head'), may hold values from 0.2 to 2
- skip_scale: float32 [32], P('head'), may hold values from 0.5 to 2
- gate_input: bfloat16 [4096, 2048], P('tok', 'head'), may hold values from -500 to 500
- norm_gain: float32 [2048], P('head'), may hold values from 0.5 to 1.5
Outputs:
- mixer_out: bfloat16 [4096, 2048], P('tok', 'head')
Inputs may be any that keep to these rules, and one draw needn't show every extreme that they name: `log_decay`: every entry is negative.
All inputs are finite; a program needn't handle non-finite values.
Results may differ from a plain program's by a relative error of at most 0.0038.
Values sent between devices are 32-bit elements; how exact they have to be, the bound alone decides.
A program may use at most 64 MiB of HBM per device.

v0:
```python
import jax
import jax.numpy as jnp
from jax import lax
from jax.sharding import PartitionSpec as P

epsilon = 1e-05


def partner_2(block, axis, distance):
    count = lax.axis_size(axis)
    route = []
    for low in range(count):
        high = low | 1 << distance
        if high != low and high < count:
            route += [(low, high), (high, low)]
    return lax.ppermute(block, axis, route)


def block_levels(row_count, col_count, local_bits):
    query_pos = jnp.arange(row_count, dtype=jnp.int32)
    key_pos = jnp.arange(col_count, dtype=jnp.int32)
    crossing = jnp.bitwise_xor(query_pos[:, None], key_pos[None, :])
    level_map = jnp.zeros((row_count, col_count), jnp.int32)
    for shift_bit in range(local_bits):
        level_map = level_map + (crossing >= 1 << shift_bit).astype(jnp.int32)
    return (level_map, key_pos[None, :] <= query_pos[:, None])


def local_mix(queries, key_rows, values, decays, scales, local_bits):
    block_len = queries.shape[0]
    row_block = min(512, block_len)
    scores = jnp.dot(queries, key_rows.T, preferred_element_type=jnp.float32)
    level_map, causal = block_levels(row_block, row_block, local_bits)

    def local_one_head(inputs):
        decay_row, scale_row, value_row = inputs
        spread = jnp.where(
            causal, decay_row[0:row_block, None] - decay_row[None, :row_block], -jnp.inf
        )
        chosen = jnp.zeros((row_block, row_block), jnp.float32)
        for level_index in range(local_bits + 1):
            chosen = chosen + jnp.where(
                level_map == level_index, scale_row[0:row_block, level_index : level_index + 1], 0.0
            )
        weighted = (scores * jnp.exp(spread) * chosen).astype(jnp.bfloat16)
        return jnp.dot(weighted, value_row, preferred_element_type=jnp.float32)

    pieces_out = lax.map(local_one_head, (decays, scales, values))
    return pieces_out


def make_state(key_rows, values, decays):
    scaled = (
        key_rows.astype(jnp.float32)[None] * jnp.exp(decays[:, -1:] - decays)[:, :, None]
    ).astype(jnp.bfloat16)
    return jnp.einsum("htn,htp->hnp", scaled, values, preferred_element_type=jnp.float32)


def far_mix(queries, decays, scales, crossed, first_level):
    query_wide = queries.astype(jnp.float32)
    tree_bits = crossed.shape[1]

    def far_one_head(inputs):
        decay_row, scale_row, state_row = inputs
        stacked = state_row.transpose(1, 0, 2).reshape(state_row.shape[1], -1)
        readout = jnp.dot(query_wide, stacked, precision=lax.Precision.HIGHEST).reshape(
            query_wide.shape[0], tree_bits, -1
        )
        level_scale = scale_row[:, first_level : first_level + tree_bits]
        return jnp.exp(decay_row)[:, None] * jnp.sum(level_scale[:, :, None] * readout, axis=1)

    return lax.map(far_one_head, (decays, scales, crossed))


def head_mix(queries, key_rows, values, decays, scales, crossed, gates, skip_scale, local_bits):
    nearby = local_mix(queries, key_rows, values, decays, scales, local_bits)
    distant = far_mix(queries, decays, scales, crossed, local_bits + 1)
    mixed_out = nearby + distant + skip_scale[:, None, None] * values.astype(jnp.float32)
    head_count, block_len, head_size = mixed_out.shape
    mixed_out = mixed_out.transpose(1, 0, 2).reshape(block_len, head_count * head_size)
    return mixed_out * jax.nn.silu(gates.astype(jnp.float32))


def shards(
    head_inputs,
    state_keys,
    state_queries,
    log_decay,
    level_weight,
    skip_scale,
    gate_input,
    norm_gain,
):
    block_len = head_inputs.shape[0]
    head_count = log_decay.shape[1]
    head_size = head_inputs.shape[1] // head_count
    local_bits = block_len.bit_length() - 1
    tree_bits = lax.axis_size("tok").bit_length() - 1
    head_values = head_inputs.reshape(block_len, head_count, head_size).transpose(1, 0, 2)
    decay_sum = jnp.cumsum(log_decay, axis=0).T
    weights = level_weight.transpose(1, 0, 2)
    block_state = make_state(state_keys, head_values, decay_sum)
    block_total = decay_sum[:, -1]
    position = lax.axis_index("tok")
    aggregate = block_state
    extent = block_total
    leading = jnp.zeros_like(block_total)
    collected = []
    for level_bit in range(tree_bits):
        partner, partner_extent = partner_2((aggregate, extent), "tok", level_bit)
        upper_half = jnp.bitwise_and(jnp.right_shift(position, level_bit), 1) == 1
        collected.append(jnp.where(upper_half, partner * jnp.exp(leading)[:, None, None], 0.0))
        merged_upper = partner * jnp.exp(extent)[:, None, None] + aggregate
        merged_lower = aggregate * jnp.exp(partner_extent)[:, None, None] + partner
        aggregate = jnp.where(upper_half, merged_upper, merged_lower)
        leading = jnp.where(upper_half, leading + partner_extent, leading)
        extent = extent + partner_extent
    crossed = jnp.stack(collected, axis=0)
    crossed = crossed.transpose(1, 0, 2, 3)
    gated_out = head_mix(
        state_queries,
        state_keys,
        head_values,
        decay_sum,
        weights,
        crossed,
        gate_input,
        skip_scale,
        local_bits,
    )
    squares = lax.psum(jnp.sum(gated_out * gated_out, axis=1), "head")
    norm_width = head_count * head_size * lax.axis_size("head")
    scaling = lax.rsqrt(squares / norm_width + epsilon)
    return (gated_out * scaling[:, None] * norm_gain[None, :]).astype(jnp.bfloat16)


def solution(mesh):
    return jax.shard_map(
        shards,
        mesh=mesh,
        in_specs=(
            P("tok", "head"),
            P("tok", None),
            P("tok", None),
            P("tok", "head"),
            P("tok", "head", None),
            P("head"),
            P("tok", "head"),
            P("head"),
        ),
        out_specs=P("tok", "head"),
        check_vma=False,
    )
```

profile of v0, /device:TPU:0, one launch (start us, length us, event | category | flops | bytes accessed | tf_op | source)
XLA Modules:
  0.0 69.3 jit_solution(14456564480159418063)
XLA Ops:
  0.0 2.2 %reduce-window.6 = f32[8,4,128]{2,0,1:T(8,128)S(1)} reduce-window(f32[8,4,128]{2,0,1:T(8,128)} %bitcast.129, f32[]{:T(128)} %constant.19.clone.1), window={size=1x1x128 pad=0_0x0_0x127_0}, to_apply=%region_0.0 | reduce-window | flops 520192 | bytes 32772 | tf_op jit(solution)/shard_map/reduce-window
  2.2 0.2 slice_reduce_fusion
  2.4 0.1 add_bitcast_fusion
  2.5 0.2 slice_reduce_fusion.1
  2.7 3.0 %collective-permute-start.1 = (f32[8]{0:T(128)S(1)}, f32[8]{0:T(128)S(1)}, u32[]{:S(2)}, u32[]{:S(2)}) collective-permute-start(f32[8]{0:T(128)S(1)} %slice_reduce_fusion.1), channel_id=1, source_target_pairs={{0,4},{4,0},{8,12},{12,8},{16,20},{20,16},{24,28},{28,24},{1,5},{5... | collective-permute-start | bytes 104 | tf_op jit(solution)/shard_map/ppermute | solution.py:16
  5.7 0.1 subtract_exponential_fusion
  5.8 1.3 %copy.25 = bf16[512,512]{0,1:T(8,128)(2,1)S(1)} copy(bf16[512,512]{1,0:T(8,128)(2,1)} %param.12) | data formatting | bytes 1048576 | tf_op args[0]
  7.1 0.8 %fusion.67 = f32[8,128,64]{1,2,0:T(8,128)S(1)} fusion(bf16[8,512,64]{1,2,0:T(8,128)(2,1)S(1)} %bitcast.114, f32[8,512]{1,0:T(8,128)S(1)} %subtract_exponential_fusion, f32[512,128]{1,0:T(8,128)S(1)} %convert_element_type.219), kind=kOutput, calls=%fused_computation.80 | convolution fusion | flops 68157440 | bytes 1064960 | tf_op jit(solution)/shard_map/htn,htp->hnp/dot_general | solution.py:56
  7.9 0.1 collective-permute-start
  8.0 0.6 fusion.72
  8.6 2.1 %collective-permute-start.3 = (f32[8]{0:T(128)S(1)}, f32[8]{0:T(128)S(1)}, u32[]{:S(2)}, u32[]{:S(2)}) collective-permute-start(f32[8]{0:T(128)S(1)} %get-tuple-element.212), channel_id=1, source_target_pairs={{0,8},{8,0},{4,12},{12,4},{16,24},{24,16},{20,28},{28,20},{1,9},{9... | collective-permute-start | bytes 104 | tf_op jit(solution)/shard_map/ppermute | solution.py:16
  10.7 1.5 %collective-permute-done.3 = f32[8]{0:T(128)S(1)} collective-permute-done((f32[8]{0:T(128)S(1)}, f32[8]{0:T(128)S(1)}, u32[]{:S(2)}, u32[]{:S(2)}) %collective-permute-start.3) | collective-permute-done | bytes 64 | tf_op jit(solution)/shard_map/ppermute | solution.py:16
  12.2 0.6 fusion.71
  12.8 2.9 %collective-permute-done = f32[8,128,64]{1,2,0:T(8,128)S(1)} collective-permute-done((f32[8,128,64]{1,2,0:T(8,128)S(1)}, f32[8,128,64]{1,2,0:T(8,128)S(1)}, u32[]{:S(2)}, u32[]{:S(2)}) %collective-permute-start) | collective-permute-done | bytes 262176 | tf_op jit(solution)/shard_map/ppermute | solution.py:16
  15.7 0.1 select_bitcast_fusion.2
  15.8 1.6 %collective-permute-start.2 = (f32[8,128,64]{1,2,0:T(8,128)S(1)}, f32[8,128,64]{1,2,0:T(8,128)S(1)}, u32[]{:S(2)}, u32[]{:S(2)}) collective-permute-start(f32[8,128,64]{1,2,0:T(8,128)S(1)} %get-tuple-element.224), channel_id=1, source_target_pairs={{0,8},{8,0},{4,12},{12,4},{16,24},{24,16},{20,28},{28,20},{1,9},{9... | collective-permute-start | bytes 786440 | tf_op jit(solution)/shard_map/ppermute | solution.py:16
  17.5 0.2 copy.33
  17.7 0.3 fusion.75
  18.0 4.8 %collective-permute-done.2 = f32[8,128,64]{1,2,0:T(8,128)S(1)} collective-permute-done((f32[8,128,64]{1,2,0:T(8,128)S(1)}, f32[8,128,64]{1,2,0:T(8,128)S(1)}, u32[]{:S(2)}, u32[]{:S(2)}) %collective-permute-start.2) | collective-permute-done | bytes 262176 | tf_op jit(solution)/shard_map/ppermute | solution.py:16
  22.8 0.8 %select_bitcast_fusion.1 = (f32[1,8,128,64]{2,3,1,0:T(8,128)S(1)}, f32[8,128,64]{1,2,0:T(8,128)S(1)}) fusion(f32[8,128,64]{1,2,0:T(8,128)S(1)} %collective-permute-done.2, f32[8]{0:T(128)} %get-tuple-element.227, pred[]{:T(512)S(6)} %eq.40, f32[8,128,64]{1,2,0:T(8,128)S(1)} %get-tuple-element.224, f32[8]{0:T(128)} %get-tuple-element.229, f32[8]{0:T(128)} %get-tuple-element.211), kind=kLoop, calls=%fused_computation.90 | loop fusion | flops 458752 | bytes 1048673 | tf_op jit(solution)/shard_map/stack | solution.py:118
  23.6 2.7 %collective-permute-start.4 = (f32[8,128,64]{1,2,0:T(8,128)S(1)}, f32[8,128,64]{1,2,0:T(8,128)S(1)}, u32[]{:S(2)}, u32[]{:S(2)}) collective-permute-start(f32[8,128,64]{1,2,0:T(8,128)S(1)} %get-tuple-element.226), channel_id=1, source_target_pairs={{0,16},{16,0},{4,20},{20,4},{8,24},{24,8},{12,28},{28,12},{1,17},{... | collective-permute-start | bytes 786440 | tf_op jit(solution)/shard_map/ppermute | solution.py:16
  26.3 1.1 %broadcast.92.clone = f32[8,512,64]{1,2,0:T(8,128)} broadcast(f32[]{:T(128)} %constant.19.clone.1), dimensions={} | broadcast | bytes 1048580 | tf_op jit(solution)/shard_map/broadcast.28
  27.4 26.1 %while.23 = (s32[]{:T(128)}, f32[8,512,64]{1,2,0:T(8,128)}, f32[8,512]{1,0:T(8,128)S(1)}, f32[512,512]{1,0:T(8,128)S(1)}, f32[8,512,18]{1,2,0:T(8,128)S(1)}, /*index=5*/bf16[8,512,64]{1,2,0:T(8,128)(2,1)S(1)}, s32[]{:T(128)}) while((s32[]{:T(128)}, f32[8,512,64]{1,2,0:T(8,128)}, f32[8,512]{1,0:T(8,128)S(1)}, ...), condition=%wide.region_3.4_spmd.clone.clone, body=%wide.region_2.3_spmd.clone.clone.sunk | while | flops 49807360 | bytes 1389653 | solution.py:48
  27.4 3.2 %fusion.94 = f32[8,512,64]{1,2,0:T(8,128)} fusion(f32[8,512,64]{1,2,0:T(8,128)} %get-tuple-element.334, s32[]{:T(128)} %get-tuple-element.333, f32[512,512]{1,0:T(8,128)S(1)} %get-tuple-element.343, f32[512]{0:T(512)S(1)} %bitcast.119, f32[512]{0:T(512)S(1)} %bitcast.120, f32[512]{0:T(512)S(1)} %bitcast.121, f32[512]{0:T(512)S(1)} %bitcast.122, ...), kind=kOutput, calls=%fused_computation.9.clone.1 | convolution fusion | flops 49807360 | bytes 1270784 | tf_op jit(solution)/shard_map/while/body/eval_jaxpr/dot_general | solution.py:46
  30.7 3.2 %fusion.94 = f32[8,512,64]{1,2,0:T(8,128)} fusion(f32[8,512,64]{1,2,0:T(8,128)} %get-tuple-element.334, s32[]{:T(128)} %get-tuple-element.333, f32[512,512]{1,0:T(8,128)S(1)} %get-tuple-element.343, f32[512]{0:T(512)S(1)} %bitcast.119, f32[512]{0:T(512)S(1)} %bitcast.120, f32[512]{0:T(512)S(1)} %bitcast.121, f32[512]{0:T(512)S(1)} %bitcast.122, ...), kind=kOutput, calls=%fused_computation.9.clone.1 | convolution fusion | flops 49807360 | bytes 1270784 | tf_op jit(solution)/shard_map/while/body/eval_jaxpr/dot_general | solution.py:46
  33.9 3.2 %fusion.94 = f32[8,512,64]{1,2,0:T(8,128)} fusion(f32[8,512,64]{1,2,0:T(8,128)} %get-tuple-element.334, s32[]{:T(128)} %get-tuple-element.333, f32[512,512]{1,0:T(8,128)S(1)} %get-tuple-element.343, f32[512]{0:T(512)S(1)} %bitcast.119, f32[512]{0:T(512)S(1)} %bitcast.120, f32[512]{0:T(512)S(1)} %bitcast.121, f32[512]{0:T(512)S(1)} %bitcast.122, ...), kind=kOutput, calls=%fused_computation.9.clone.1 | convolution fusion | flops 49807360 | bytes 1270784 | tf_op jit(solution)/shard_map/while/body/eval_jaxpr/dot_general | solution.py:46
  37.2 3.2 %fusion.94 = f32[8,512,64]{1,2,0:T(8,128)} fusion(f32[8,512,64]{1,2,0:T(8,128)} %get-tuple-element.334, s32[]{:T(128)} %get-tuple-element.333, f32[512,512]{1,0:T(8,128)S(1)} %get-tuple-element.343, f32[512]{0:T(512)S(1)} %bitcast.119, f32[512]{0:T(512)S(1)} %bitcast.120, f32[512]{0:T(512)S(1)} %bitcast.121, f32[512]{0:T(512)S(1)} %bitcast.122, ...), kind=kOutput, calls=%fused_computation.9.clone.1 | convolution fusion | flops 49807360 | bytes 1270784 | tf_op jit(solution)/shard_map/while/body/eval_jaxpr/dot_general | solution.py:46
  40.5 3.2 %fusion.94 = f32[8,512,64]{1,2,0:T(8,128)} fusion(f32[8,512,64]{1,2,0:T(8,128)} %get-tuple-element.334, s32[]{:T(128)} %get-tuple-element.333, f32[512,512]{1,0:T(8,128)S(1)} %get-tuple-element.343, f32[512]{0:T(512)S(1)} %bitcast.119, f32[512]{0:T(512)S(1)} %bitcast.120, f32[512]{0:T(512)S(1)} %bitcast.121, f32[512]{0:T(512)S(1)} %bitcast.122, ...), kind=kOutput, calls=%fused_computation.9.clone.1 | convolution fusion | flops 49807360 | bytes 1270784 | tf_op jit(solution)/shard_map/while/body/eval_jaxpr/dot_general | solution.py:46
  43.7 3.2 %fusion.94 = f32[8,512,64]{1,2,0:T(8,128)} fusion(f32[8,512,64]{1,2,0:T(8,128)} %get-tuple-element.334, s32[]{:T(128)} %get-tuple-element.333, f32[512,512]{1,0:T(8,128)S(1)} %get-tuple-element.343, f32[512]{0:T(512)S(1)} %bitcast.119, f32[512]{0:T(512)S(1)} %bitcast.120, f32[512]{0:T(512)S(1)} %bitcast.121, f32[512]{0:T(512)S(1)} %bitcast.122, ...), kind=kOutput, calls=%fused_computation.9.clone.1 | convolution fusion | flops 49807360 | bytes 1270784 | tf_op jit(solution)/shard_map/while/body/eval_jaxpr/dot_general | solution.py:46
  47.0 3.2 %fusion.94 = f32[8,512,64]{1,2,0:T(8,128)} fusion(f32[8,512,64]{1,2,0:T(8,128)} %get-tuple-element.334, s32[]{:T(128)} %get-tuple-element.333, f32[512,512]{1,0:T(8,128)S(1)} %get-tuple-element.343, f32[512]{0:T(512)S(1)} %bitcast.119, f32[512]{0:T(512)S(1)} %bitcast.120, f32[512]{0:T(512)S(1)} %bitcast.121, f32[512]{0:T(512)S(1)} %bitcast.122, ...), kind=kOutput, calls=%fused_computation.9.clone.1 | convolution fusion | flops 49807360 | bytes 1270784 | tf_op jit(solution)/shard_map/while/body/eval_jaxpr/dot_general | solution.py:46
  50.2 3.2 %fusion.94 = f32[8,512,64]{1,2,0:T(8,128)} fusion(f32[8,512,64]{1,2,0:T(8,128)} %get-tuple-element.334, s32[]{:T(128)} %get-tuple-element.333, f32[512,512]{1,0:T(8,128)S(1)} %get-tuple-element.343, f32[512]{0:T(512)S(1)} %bitcast.119, f32[512]{0:T(512)S(1)} %bitcast.120, f32[512]{0:T(512)S(1)} %bitcast.121, f32[512]{0:T(512)S(1)} %bitcast.122, ...), kind=kOutput, calls=%fused_computation.9.clone.1 | convolution fusion | flops 49807360 | bytes 1270784 | tf_op jit(solution)/shard_map/while/body/eval_jaxpr/dot_general | solution.py:46
  53.5 1.3 %copy.28 = bf16[512,512]{0,1:T(8,128)(2,1)S(1)} copy(bf16[512,512]{1,0:T(8,128)(2,1)} %param.18) | data formatting | bytes 1048576 | tf_op args[6]
  54.8 0.1 select_bitcast_fusion
  55.0 0.1 broadcast.92.clone.1
  55.1 5.2 %while.22 = (s32[]{:T(128)}, f32[8,512,64]{1,2,0:T(8,128)S(1)}, f32[8,512]{1,0:T(8,128)S(1)}, f32[8,512,18]{1,2,0:T(8,128)S(1)}, f32[8,3,128,64]{2,3,0,1:T(8,128)S(1)}, /*index=5*/f32[512,128]{1,0:T(8,128)S(1)}, s32[]{:T(128)}) while((s32[]{:T(128)}, f32[8,512,64]{1,2,0:T(8,128)S(1)}, f32[8,512]{1,0:T(8,128)S(1)}, ...), condition=%wide.region_6.7_spmd, body=%wide.region_4.6_spmd.sunk | while | flops 151191552 | bytes 1835101 | solution.py:72
  55.1 0.5 fusion.90
  55.8 0.5 fusion.90
  56.4 0.5 fusion.90
  57.1 0.5 fusion.90
  57.7 0.5 fusion.90
  58.3 0.5 fusion.90
  59.0 0.5 fusion.90
  59.6 0.5 fusion.90
  60.2 1.6 %multiply_add_fusion = f32[8,512,64]{1,2,0:T(8,128)S(1)} fusion(bf16[8,512,64]{1,2,0:T(8,128)(2,1)S(1)} %get-tuple-element.368, f32[8,512,64]{1,2,0:T(8,128)} %get-tuple-element.106, f32[8,512,64]{1,2,0:T(8,128)S(1)} %get-tuple-element.107, f32[8]{0:T(128)} %param.17), kind=kLoop, calls=%fused_computation.83 | loop fusion | flops 1048576 | bytes 3670048 | tf_op jit(solution)/shard_map/add | solution.py:78
  61.8 0.4 multiply_reduce_fusion.1
  62.2 5.7 %psum.7 = f32[512]{0:T(512)S(1)} all-reduce(f32[512]{0:T(512)S(1)} %multiply_reduce_fusion.1), channel_id=1, replica_groups=mesh['tok'=8,'head'=4] {'head'}, use_global_device_ids=true, to_apply=%region_8.9 | all-reduce | flops 512 | bytes 4096 | tf_op jit(solution)/shard_map/psum | solution.py:131
  67.9 0.4 multiply_convert_fusion.4
  68.3 1.0 %copy.29 = bf16[512,512]{1,0:T(8,128)(2,1)} copy(bf16[512,512]{0,1:T(8,128)(2,1)S(1)} %multiply_convert_fusion.4) | data formatting | bytes 1048576 | tf_op jit(solution)/shard_map/convert_element_type | solution.py:134
  (90 shorter events, 1.2 us)
Async XLA Ops:
  0.0 7.0 %copy-start = (bf16[512,128]{1,0:T(8,128)(2,1)S(1)}, bf16[512,128]{1,0:T(8,128)(2,1)}, u32[]{:S(2)}) copy-start(bf16[512,128]{1,0:T(8,128)(2,1)} %param.13) | copy-start | bytes 393220
  2.7 5.3 %collective-permute-start.1 = (f32[8]{0:T(128)S(1)}, f32[8]{0:T(128)S(1)}, u32[]{:S(2)}, u32[]{:S(2)}) collective-permute-start(f32[8]{0:T(128)S(1)} %slice_reduce_fusion.1), channel_id=1, source_target_pairs={{0,4},{4,0},{8,12},{12,8},{16,20},{20,16},{24,28},{28,24},{1,5},{5... | collective-permute-start | bytes 104 | tf_op jit(solution)/shard_map/ppermute | solution.py:16
  7.1 10.4 %copy-start.2 = (f32[512,8,18]{0,1,2:T(8,128)S(1)}, f32[512,8,18]{0,1,2:T(8,128)}, u32[]{:S(2)}) copy-start(f32[512,8,18]{0,1,2:T(8,128)} %param.16) | copy-start | bytes 884740
  7.9 9.8 %copy-start.1 = (bf16[512,128]{1,0:T(8,128)(2,1)S(1)}, bf16[512,128]{1,0:T(8,128)(2,1)}, u32[]{:S(2)}) copy-start(bf16[512,128]{1,0:T(8,128)(2,1)} %param.14) | copy-start | bytes 393220
  7.9 7.8 %collective-permute-start = (f32[8,128,64]{1,2,0:T(8,128)S(1)}, f32[8,128,64]{1,2,0:T(8,128)S(1)}, u32[]{:S(2)}, u32[]{:S(2)}) collective-permute-start(f32[8,128,64]{1,2,0:T(8,128)S(1)} %fusion.67), channel_id=1, source_target_pairs={{0,4},{4,0},{8,12},{12,8},{16,20},{20,16},{24,28},{28,24},{1,5},{5... | collective-permute-start | bytes 786440 | tf_op jit(solution)/shard_map/ppermute | solution.py:16
  8.6 3.6 %collective-permute-start.3 = (f32[8]{0:T(128)S(1)}, f32[8]{0:T(128)S(1)}, u32[]{:S(2)}, u32[]{:S(2)}) collective-permute-start(f32[8]{0:T(128)S(1)} %get-tuple-element.212), channel_id=1, source_target_pairs={{0,8},{8,0},{4,12},{12,4},{16,24},{24,16},{20,28},{28,20},{1,9},{9... | collective-permute-start | bytes 104 | tf_op jit(solution)/shard_map/ppermute | solution.py:16
  15.8 6.9 %collective-permute-start.2 = (f32[8,128,64]{1,2,0:T(8,128)S(1)}, f32[8,128,64]{1,2,0:T(8,128)S(1)}, u32[]{:S(2)}, u32[]{:S(2)}) collective-permute-start(f32[8,128,64]{1,2,0:T(8,128)S(1)} %get-tuple-element.224), channel_id=1, source_target_pairs={{0,8},{8,0},{4,12},{12,4},{16,24},{24,16},{20,28},{28,20},{1,9},{9... | collective-permute-start | bytes 786440 | tf_op jit(solution)/shard_map/ppermute | solution.py:16
  23.6 31.2 %collective-permute-start.4 = (f32[8,128,64]{1,2,0:T(8,128)S(1)}, f32[8,128,64]{1,2,0:T(8,128)S(1)}, u32[]{:S(2)}, u32[]{:S(2)}) collective-permute-start(f32[8,128,64]{1,2,0:T(8,128)S(1)} %get-tuple-element.226), channel_id=1, source_target_pairs={{0,16},{16,0},{4,20},{20,4},{8,24},{24,8},{12,28},{28,12},{1,17},{... | collective-permute-start | bytes 786440 | tf_op jit(solution)/shard_map/ppermute | solution.py:16
  53.5 1.3 %copy-start.3 = (f32[8]{0:T(128)S(1)}, f32[8]{0:T(128)}, u32[]{:S(2)}) copy-start(f32[8]{0:T(128)} %get-tuple-element.228) | copy-start | bytes 100
  61.8 6.1 %copy-start.4 = (f32[512]{0:T(512)S(1)}, f32[512]{0:T(512)}, u32[]{:S(2)}) copy-start(f32[512]{0:T(512)} %param.19) | copy-start | bytes 6148
where the time goes:
time: 69.6 us; the launch traced here: 69.3 us
  matrix products  30.7 us (44%)
  starting transfers between devices  9.46 us (14%)
  waiting for transfers between devices  9.24 us (13%)
  other arithmetic  7.51 us (11%)
  local copies, waits for them, and re-layouts  5.92 us (9%)
  blocking collectives  5.66 us (8%)
    dot_general x8, matrix products, local_one_head(): return jnp.dot(weighted, value_row, preferred_element_type=jnp.float32)  25.8 us
    ppermute x5, starting transfers between devices, partner_2(): return lax.ppermute(block, axis, route)  9.46 us
    ppermute x5, waiting for transfers between devices, partner_2(): return lax.ppermute(block, axis, route)  9.24 us
    psum x1, blocking collectives, shards(): squares = lax.psum(jnp.sum(gated_out * gated_out, axis=1), 'head')  5.66 us
    dot_general x8, matrix products, far_one_head(): jnp.dot(query_wide, stacked, precision=lax.Precision.HIGHEST)  3.81 us
    unnamed x13, local copies, waits for them, and re-layouts  2.71 us
    another operation x3, other arithmetic  2.35 us
    add x1, other arithmetic, head_mix(): nearby + distant + skip_scale[:, None, None] * values.astype(jnp.float32)  1.58 us
  transfers between devices with their start and end apart: 5, of which 3 were waited for; matrix products, arithmetic and copies ran while one was open for 46% of the time, Pallas kernels for 0%

commit v1 on v0

v1 whole, which is shorter than its diff:
```python
import functools

import jax
import jax.numpy as jnp
from jax import lax
from jax.experimental import pallas as pl
from jax.experimental.pallas import tpu as pltpu
from jax.sharding import PartitionSpec as P

epsilon = 1e-05
F32, BF16 = jnp.float32, jnp.bfloat16
MESH = pl.DeviceIdType.MESH


def dot(a, b):
    return jnp.dot(a, b, preferred_element_type=F32)


def dot_t(a, b):
    return lax.dot_general(a, b, (((1,), (1,)), ((), ())), preferred_element_type=F32)


def bit_of(value, b):
    return lax.rem(lax.div(value, 1 << b), 2) == 1


def column(row, size):
    return jnp.broadcast_to(row, (size, size)).T


def level_of(crossing, bits):
    level = jnp.zeros(crossing.shape, jnp.int32)
    for b in range(bits):
        level = level + (crossing >= 1 << b).astype(jnp.int32)
    return level


def kernel(
    sizes,
    x_ref, k_ref, q_ref, ld_ref, w_ref, skip_ref, gate_ref, gain_ref,
    out_ref,
    d_ref, tot, fac_lead, fac_all, state, agg, got, base, sg, vt, gt, kt, qq, score, turned, ssq,
    tot_send, tot_recv, st_send, st_recv, sq_send, sq_recv,
):
    toks, heads_ax, tile, chunks = sizes
    block, width = x_ref.shape
    heads = ld_ref.shape[0]
    size = width // heads
    local_bits = block.bit_length() - 1
    tree = toks.bit_length() - 1
    tiles = block // tile
    tile_bits = tile.bit_length() - 1
    per = heads // chunks
    rows = per * size
    me = lax.axis_index("tok")
    my_head = lax.axis_index("head")
    odd = lax.rem(me, 2) == 1
    partner = me + 1 - 2 * lax.rem(me, 2)

    barrier = pltpu.get_barrier_semaphore()
    for i in range(1, toks):
        pl.semaphore_signal(barrier, inc=1, device_id={"tok": lax.rem(me + i, toks)}, device_id_type=MESH)
    for i in range(1, heads_ax):
        pl.semaphore_signal(barrier, inc=1, device_id={"head": lax.rem(my_head + i, heads_ax)}, device_id_type=MESH)

    ones = (
        lax.broadcasted_iota(jnp.int32, (tile, tile), 0) <= lax.broadcasted_iota(jnp.int32, (tile, tile), 1)
    ).astype(F32)
    inside = jnp.dot(
        jnp.concatenate([ld_ref[:, i * tile : (i + 1) * tile] for i in range(tiles)], axis=0),
        ones, precision=lax.Precision.HIGHEST, preferred_element_type=F32,
    )
    run = jnp.zeros((heads, 1), F32)
    for i in range(tiles):
        part = inside[i * heads : (i + 1) * heads] + run
        d_ref[:, i * tile : (i + 1) * tile] = part
        run = part[:, tile - 1 :]
    tot[me] = jnp.broadcast_to(run, tot.shape[1:])
    pl.semaphore_wait(barrier, toks - 1 + heads_ax - 1)

    def tot_copy(peer, slot):
        return pltpu.make_async_remote_copy(
            src_ref=tot.at[slot], dst_ref=tot.at[slot], send_sem=tot_send.at[peer], recv_sem=tot_recv.at[slot],
            device_id={"tok": peer}, device_id_type=MESH,
        )

    for i in range(1, toks):
        tot_copy(lax.rem(me + i, toks), me).start()

    def state_copy(src, b, c, peer):
        part = pl.ds(c * rows, rows)
        return pltpu.make_async_remote_copy(
            src_ref=src.at[part], dst_ref=got.at[b, part], send_sem=st_send.at[b, c], recv_sem=st_recv.at[b, c],
            device_id={"tok": peer}, device_id_type=MESH,
        )

    vt[...] = x_ref[...].T
    kt[...] = k_ref[...].T.astype(F32)
    to_end = jnp.exp(run - d_ref[...])
    for c in range(chunks):
        for h in range(c * per, (c + 1) * per):
            scaled = (kt[...] * to_end[h : h + 1]).astype(BF16)
            state[h * size : (h + 1) * size] = dot_t(vt[h * size : (h + 1) * size], scaled)
        state_copy(state, 0, c, partner).start()

    gt[...] = gate_ref[...].T
    qt = q_ref[...].T
    depth = qt.shape[0]
    qq[:depth] = qt
    qq[depth:] = qt
    score[...] = dot_t(k_ref[...], q_ref[...])

    groups = tile // 8
    t_at = lax.broadcasted_iota(jnp.int32, (groups, tile), 1)
    g_at = lax.broadcasted_iota(jnp.int32, (groups, tile), 0)
    coarse = jnp.where(t_at // 8 > g_at, level_of((t_at // 8) ^ g_at, tile_bits - 3) + 3, -1)
    same = (t_at // 8 == g_at).astype(F32).reshape(groups, 1, tile) > 0.5
    r_at = lax.broadcasted_iota(jnp.int32, (8, tile), 0)
    u_at = lax.broadcasted_iota(jnp.int32, (8, tile), 1) % 8
    fine = jnp.where(u_at >= r_at, level_of(u_at ^ r_at, 3), -1)

    def near(h, _):
        lines = pl.ds(pl.multiple_of(h * size, size), size)
        decay = d_ref[pl.ds(h, 1), :]
        weight = [w_ref[l, pl.ds(h, 1), :] for l in range(local_bits + 1)]
        cut = [slice(i * tile, (i + 1) * tile) for i in range(tiles)]
        made = {}
        for j in range(tiles):
            at_s = column(decay[:, cut[j]], tile)
            rough = jnp.zeros((groups, tile), F32)
            for l in range(4, tile_bits + 1):
                rough = jnp.where(coarse == l, weight[l][:, cut[j]], rough)
            exact = jnp.zeros((8, tile), F32)
            for l in range(4):
                exact = jnp.where(fine == l, weight[l][:, cut[j]], exact)
            chosen = jnp.where(
                jnp.broadcast_to(same, (groups, 8, tile)),
                jnp.broadcast_to(exact[None], (groups, 8, tile)),
                jnp.broadcast_to(rough[:, None, :], (groups, 8, tile)),
            ).reshape(tile, tile)
            spread = jnp.exp(jnp.minimum(decay[:, cut[j]] - at_s, 0.0))
            made[j, j] = (score[cut[j], cut[j]] * spread * chosen).astype(BF16)
            if j + 1 < tiles:
                last = decay[:, (j + 1) * tile - 1 : (j + 1) * tile]
                fall = jnp.exp(last - at_s)
                for i in range(j + 1, tiles):
                    by = weight[(i ^ j).bit_length() + tile_bits][:, cut[i]] * jnp.exp(decay[:, cut[i]] - last)
                    made[j, i] = (score[cut[j], cut[i]] * fall * by).astype(BF16)
        v = vt[lines, :]
        parts = []
        empty = jnp.zeros((tile, tile), BF16)
        pair = min(2, tiles)
        for i in range(0, tiles, pair):
            cols = [
                jnp.concatenate([made.get((j, ii), empty) for j in range(i + pair)], axis=0)
                for ii in range(i, i + pair)
            ]
            parts.append(dot(v[:, : (i + pair) * tile], jnp.concatenate(cols, axis=1)))
        g = gt[lines, :].astype(F32)
        g = g / (1.0 + jnp.exp(-g))
        sg[lines, :] = g
        base[lines, :] = (jnp.concatenate(parts, axis=1) + skip_ref[h] * v.astype(F32)) * g
        return 0

    def receives(b):
        return bit_of(me, b)

    def sends(b):
        return jnp.logical_and(me + 2 < toks, bit_of(me + 2, b))

    def all_ones(first, last):
        value = me >= 0
        for b in range(first, last):
            value = jnp.logical_and(value, bit_of(me, b))
        return value

    def send_own(b, c):
        if b < tree:

            @pl.when(jnp.logical_and(jnp.logical_not(bit_of(me, b)), jnp.logical_and(sends(b), all_ones(1, b))))
            def _():
                state_copy(agg, b, c, lax.rem(me + 2, toks)).start()

    def comm(b, c):
        def each(fn):
            for h in range(c * per, (c + 1) * per):
                fn(h, slice(h * size, (h + 1) * size))

        if b == 0:
            state_copy(state, 0, c, partner).wait_recv()

            def join(h, s):
                mine, other = state[s], got[0, s]
                agg[s] = jnp.where(odd, other, mine) * fac_all[0, h : h + 1, :] + jnp.where(odd, mine, other)

            if tree > 1:
                each(join)
            send_own(1, c)
        else:

            @pl.when(receives(b))
            def _():
                state_copy(agg, b, c, lax.rem(me + 2, toks)).wait_recv()

                @pl.when(sends(b))
                def _():
                    state_copy(got.at[b], b, c, lax.rem(me + 2, toks)).start()

                if b + 1 < tree:

                    @pl.when(all_ones(1, b + 1))
                    def _():
                        def join(h, s):
                            agg[s] = got[b, s] * fac_all[b, h : h + 1, :] + agg[s]

                        each(join)
                        send_own(b + 1, c)

    def distant(b, c):
        @pl.when(receives(b))
        def _():
            s = slice(c * rows, (c + 1) * rows)
            lead = jnp.concatenate(
                [jnp.broadcast_to(fac_lead[b, h : h + 1, :], (size, depth)) for h in range(c * per, (c + 1) * per)], 0
            )
            x = got[b, s] * lead
            high = x.astype(BF16)
            low = (x - high.astype(F32)).astype(BF16)
            read = dot(jnp.concatenate([high, low], axis=1), qq[...])
            for h in range(per):
                hh = c * per + h
                by = w_ref[local_bits + 1 + b, hh : hh + 1, :] * jnp.exp(d_ref[hh : hh + 1, :])
                o = slice(hh * size, (hh + 1) * size)
                base[o] += read[h * size : (h + 1) * size] * by * sg[o]

    for k in range(chunks + tree - 1):
        if k < chunks:
            lax.fori_loop(k * per, (k + 1) * per, near, 0)
        if k == 0:
            for i in range(1, toks):
                tot_copy(me, lax.rem(me + i, toks)).wait_recv()
            for b in range(tree):
                start = lax.div(me, 1 << b) * (1 << b)
                lead = jnp.zeros(tot.shape[1:], F32)
                full = lead
                low = start if b else me + 1 - lax.rem(me, 2)
                for m in range(toks):
                    one = tot[m]
                    lead = lead + jnp.where(jnp.logical_and(m >= start, m < me), one, 0.0)
                    full = full + jnp.where(jnp.logical_and(m >= low, m < low + (1 << b)), one, 0.0)
                fac_lead[b] = jnp.exp(lead)
                fac_all[b] = jnp.exp(full)
        for b in range(tree):
            if 0 <= k - b < chunks:
                comm(b, k - b)
        for b in range(tree):
            if 0 <= k - b < chunks:
                distant(b, k - b)

    total = jnp.zeros((1, block), F32)
    for h in range(heads):
        g = base[h * size : (h + 1) * size]
        total = total + jnp.sum(g * g, axis=0, keepdims=True)
    ssq[my_head] = total

    def sq_copy(peer, slot):
        return pltpu.make_async_remote_copy(
            src_ref=ssq.at[slot], dst_ref=ssq.at[slot], send_sem=sq_send.at[peer], recv_sem=sq_recv.at[slot],
            device_id={"head": peer}, device_id_type=MESH,
        )

    for i in range(1, heads_ax):
        sq_copy(lax.rem(my_head + i, heads_ax), my_head).start()
    turned[...] = base[...].T * gain_ref[...]
    for i in range(1, heads_ax):
        sq_copy(my_head, lax.rem(my_head + i, heads_ax)).wait_recv()
    squares = ssq[0]
    for m in range(1, heads_ax):
        squares = squares + ssq[m]
    scaling = lax.rsqrt(squares / (width * heads_ax) + epsilon)
    for i in range(tiles):
        s = slice(i * tile, (i + 1) * tile)
        by = column(scaling[:, s], tile)
        for j in range(width // tile):
            c = slice(j * tile, (j + 1) * tile)
            out_ref[s, c] = (turned[s, c] * by).astype(BF16)

    for i in range(1, toks):
        tot_copy(lax.rem(me + i, toks), me).wait_send()
    for i in range(1, heads_ax):
        sq_copy(lax.rem(my_head + i, heads_ax), my_head).wait_send()
    for c in range(chunks):
        state_copy(state, 0, c, partner).wait_send()
    for b in range(1, tree):

        @pl.when(jnp.logical_and(sends(b), jnp.logical_or(bit_of(me, b), all_ones(1, b))))
        def _():
            for c in range(chunks):
                state_copy(agg, b, c, lax.rem(me + 2, toks)).wait_send()


def shards(toks, heads_ax, x, k, q, ld, w, skip, gate, gain):
    block, width = x.shape
    heads = ld.shape[1]
    depth = k.shape[1]
    tree = toks.bit_length() - 1
    tile = 128
    chunks = min(4, heads)
    vmem = pl.BlockSpec(memory_space=pltpu.VMEM)
    return pl.pallas_call(
        functools.partial(kernel, (toks, heads_ax, tile, chunks)),
        out_shape=jax.ShapeDtypeStruct((block, width), BF16),
        in_specs=[vmem] * 5 + [pl.BlockSpec(memory_space=pltpu.SMEM)] + [vmem] * 2,
        out_specs=vmem,
        scratch_shapes=[
            pltpu.VMEM((heads, block), F32),
            pltpu.VMEM((toks, heads, depth), F32),
            pltpu.VMEM((tree, heads, depth), F32),
            pltpu.VMEM((tree, heads, depth), F32),
            pltpu.VMEM((width, depth), F32),
            pltpu.VMEM((width, depth), F32),
            pltpu.VMEM((tree, width, depth), F32),
            pltpu.VMEM((width, block), F32),
            pltpu.VMEM((width, block), F32),
            pltpu.VMEM((width, block), BF16),
            pltpu.VMEM((width, block), BF16),
            pltpu.VMEM((depth, block), F32),
            pltpu.VMEM((2 * depth, block), BF16),
            pltpu.VMEM((block, block), F32),
            pltpu.VMEM((block, width), F32),
            pltpu.VMEM((heads_ax, 1, block), F32),
            pltpu.SemaphoreType.DMA((toks,)),
            pltpu.SemaphoreType.DMA((toks,)),
            pltpu.SemaphoreType.DMA((tree, chunks)),
            pltpu.SemaphoreType.DMA((tree, chunks)),
            pltpu.SemaphoreType.DMA((heads_ax,)),
            pltpu.SemaphoreType.DMA((heads_ax,)),
        ],
        compiler_params=pltpu.CompilerParams(
            collective_id=0, has_side_effects=True, vmem_limit_bytes=40 * 2**20
        ),
    )(x, k, q, ld.T, w.transpose(2, 1, 0), skip, gate, gain[None, :])


def solution(mesh):
    return jax.shard_map(
        functools.partial(shards, mesh.shape["tok"], mesh.shape["head"]),
        mesh=mesh,
        in_specs=(
            P("tok", "head"),
            P("tok", None),
            P("tok", None),
            P("tok", "head"),
            P("tok", "head", None),
            P("head"),
            P("tok", "head"),
            P("head"),
        ),
        out_specs=P("tok", "head"),
        check_vma=False,
    )
```

time: 69.6 us -> 33.2 us (0.48)
  the two profiles are of different devices: /device:TPU:0 before, /device:TPU:27 now
where the time goes in v1:
time: 33.2 us; the launch traced here: 32.8 us
  Pallas kernels  25.8 us (78%)
  local copies, waits for them, and re-layouts  7.05 us (21%)
    pallas_call x1, Pallas kernels, shards(): pl.pallas_call(functools.partial(kernel, (toks, heads_ax, tile, chunks)),...  25.8 us
    unnamed x17, local copies, waits for them, and re-layouts  7.05 us

profile of v1, /device:TPU:27, one launch (start us, length us, event | category | flops | bytes accessed | tf_op | source)
XLA Modules:
  0.0 32.8 jit_solution(18140951653677902049)
XLA Ops:
  0.0 0.0 copy-start.6
  0.0 0.0 copy-start.7
  0.0 0.7 %copy-done.6 = f32[512]{0:T(512)S(1)} copy-done((f32[512]{0:T(512)S(1)}, f32[512]{0:T(512)}, u32[]{:S(2)}) %copy-start.6) | copy-done | bytes 2072
  0.7 0.0 copy-done.7
  0.7 0.0 copy-start
  0.7 1.0 %copy-done = bf16[512,512]{1,0:T(8,128)(2,1)S(1)} copy-done((bf16[512,512]{1,0:T(8,128)(2,1)S(1)}, bf16[512,512]{1,0:T(8,128)(2,1)}, u32[]{:S(2)}) %copy-start) | copy-done | bytes 524312
  1.7 0.0 copy-start.1
  1.7 1.0 %copy-done.1 = bf16[512,512]{1,0:T(8,128)(2,1)S(1)} copy-done((bf16[512,512]{1,0:T(8,128)(2,1)S(1)}, bf16[512,512]{1,0:T(8,128)(2,1)}, u32[]{:S(2)}) %copy-start.1) | copy-done | bytes 524312
  2.8 0.0 copy-start.2
  2.8 1.0 %copy-done.2 = f32[512,8,18]{0,1,2:T(8,128)S(1)} copy-done((f32[512,8,18]{0,1,2:T(8,128)S(1)}, f32[512,8,18]{0,1,2:T(8,128)}, u32[]{:S(2)}) %copy-start.2) | copy-done | bytes 294936
  3.7 0.0 copy-start.3
  3.7 0.9 %copy-done.3 = bf16[512,128]{1,0:T(8,128)(2,1)S(1)} copy-done((bf16[512,128]{1,0:T(8,128)(2,1)S(1)}, bf16[512,128]{1,0:T(8,128)(2,1)}, u32[]{:S(2)}) %copy-start.3) | copy-done | bytes 131096
  4.6 0.0 copy-start.4
  4.6 0.9 %copy-done.4 = bf16[512,128]{1,0:T(8,128)(2,1)S(1)} copy-done((bf16[512,128]{1,0:T(8,128)(2,1)S(1)}, bf16[512,128]{1,0:T(8,128)(2,1)}, u32[]{:S(2)}) %copy-start.4) | copy-done | bytes 131096
  5.5 0.0 copy-start.5
  5.5 0.7 %copy-done.5 = f32[512,8]{0,1:T(8,128)S(1)} copy-done((f32[512,8]{0,1:T(8,128)S(1)}, f32[512,8]{0,1:T(8,128)}, u32[]{:S(2)}) %copy-start.5) | copy-done | bytes 16408
  6.3 25.8 %shard_map.82 = bf16[512,512]{1,0:T(8,128)(2,1)S(1)} custom-call(bf16[512,512]{1,0:T(8,128)(2,1)S(1)} %copy-done, bf16[512,128]{1,0:T(8,128)(2,1)S(1)} %copy-done.3, bf16[512,128]{1,0:T(8,128)(2,1)S(1)} %copy-done.4, f32[8,512]{1,0:T(8,128)S(1)} %bitcast.4, f32[18,8,512]{2,1,0:T(8,128)S(1)} %bitcast.3, f32[8]{0:T(128)S(1)} %copy-done.7, ...), custom_call_target="tpu_custom_call" | custom-call | tf_op jit(solution)/shard_map/pallas_call | solution.py:310
  32.0 0.8 %copy.10 = bf16[512,512]{1,0:T(8,128)(2,1)} copy(bf16[512,512]{1,0:T(8,128)(2,1)S(1)} %shard_map.82) | data formatting | bytes 1048576
Async XLA Ops:
  0.0 0.7 %copy-start.6 = (f32[512]{0:T(512)S(1)}, f32[512]{0:T(512)}, u32[]{:S(2)}) copy-start(f32[512]{0:T(512)} %param.15) | copy-start | bytes 6148
  0.0 0.7 %copy-start.7 = (f32[8]{0:T(128)S(1)}, f32[8]{0:T(128)}, u32[]{:S(2)}) copy-start(f32[8]{0:T(128)} %skip_ref.1) | copy-start | bytes 100
  0.7 1.0 %copy-start = (bf16[512,512]{1,0:T(8,128)(2,1)S(1)}, bf16[512,512]{1,0:T(8,128)(2,1)}, u32[]{:S(2)}) copy-start(bf16[512,512]{1,0:T(8,128)(2,1)} %x_ref.1) | copy-start | bytes 1572868
  1.7 1.0 %copy-start.1 = (bf16[512,512]{1,0:T(8,128)(2,1)S(1)}, bf16[512,512]{1,0:T(8,128)(2,1)}, u32[]{:S(2)}) copy-start(bf16[512,512]{1,0:T(8,128)(2,1)} %gate_ref.1) | copy-start | bytes 1572868
  2.8 1.0 %copy-start.2 = (f32[512,8,18]{0,1,2:T(8,128)S(1)}, f32[512,8,18]{0,1,2:T(8,128)}, u32[]{:S(2)}) copy-start(f32[512,8,18]{0,1,2:T(8,128)} %param.12) | copy-start | bytes 884740
  3.7 0.9 %copy-start.3 = (bf16[512,128]{1,0:T(8,128)(2,1)S(1)}, bf16[512,128]{1,0:T(8,128)(2,1)}, u32[]{:S(2)}) copy-start(bf16[512,128]{1,0:T(8,128)(2,1)} %k_ref.1) | copy-start | bytes 393220
  4.6 0.9 %copy-start.4 = (bf16[512,128]{1,0:T(8,128)(2,1)S(1)}, bf16[512,128]{1,0:T(8,128)(2,1)}, u32[]{:S(2)}) copy-start(bf16[512,128]{1,0:T(8,128)(2,1)} %q_ref.1) | copy-start | bytes 393220
  5.5 0.7 %copy-start.5 = (f32[512,8]{0,1:T(8,128)S(1)}, f32[512,8]{0,1:T(8,128)}, u32[]{:S(2)}) copy-start(f32[512,8]{0,1:T(8,128)} %param.11) | copy-start | bytes 49156

commit v2 on v1

--- a/solution.py
+++ b/solution.py
@@ -37,12 +37,24 @@
 
 def kernel(
     sizes,
-    x_ref, k_ref, q_ref, ld_ref, w_ref, skip_ref, gate_ref, gain_ref,
+    x_in, k_in, q_in, ld_in, w_in, skip_ref, gate_in, gain_ref,
     out_ref,
+    x_ref, k_ref, q_ref, ld_ref, w_ref, gate_ref, load_sem,
     d_ref, tot, fac_lead, fac_all, state, agg, got, base, sg, vt, gt, kt, qq, score, turned, ssq,
     tot_send, tot_recv, st_send, st_recv, sq_send, sq_recv,
 ):
     toks, heads_ax, tile, chunks = sizes
+    loads = {
+        name: pltpu.make_async_copy(src, dst, load_sem.at[i])
+        for i, (name, src, dst) in enumerate(
+            (
+                ("ld", ld_in, ld_ref), ("k", k_in, k_ref), ("x", x_in, x_ref),
+                ("q", q_in, q_ref), ("gate", gate_in, gate_ref), ("w", w_in, w_ref),
+            )
+        )
+    }
+    for load in loads.values():
+        load.start()
     block, width = x_ref.shape
     heads = ld_ref.shape[0]
     size = width // heads
@@ -63,20 +75,24 @@
     for i in range(1, heads_ax):
         pl.semaphore_signal(barrier, inc=1, device_id={"head": lax.rem(my_head + i, heads_ax)}, device_id_type=MESH)
 
-    ones = (
-        lax.broadcasted_iota(jnp.int32, (tile, tile), 0) <= lax.broadcasted_iota(jnp.int32, (tile, tile), 1)
-    ).astype(F32)
-    inside = jnp.dot(
-        jnp.concatenate([ld_ref[:, i * tile : (i + 1) * tile] for i in range(tiles)], axis=0),
-        ones, precision=lax.Precision.HIGHEST, preferred_element_type=F32,
-    )
-    run = jnp.zeros((heads, 1), F32)
-    for i in range(tiles):
-        part = inside[i * heads : (i + 1) * heads] + run
-        d_ref[:, i * tile : (i + 1) * tile] = part
-        run = part[:, tile - 1 :]
+    with jax.named_scope("running_sum"):
+        loads["ld"].wait()
+        ones = (
+            lax.broadcasted_iota(jnp.int32, (tile, tile), 0) <= lax.broadcasted_iota(jnp.int32, (tile, tile), 1)
+        ).astype(F32)
+        inside = jnp.dot(
+            jnp.concatenate([ld_ref[:, i * tile : (i + 1) * tile] for i in range(tiles)], axis=0),
+            ones, precision=lax.Precision.HIGHEST, preferred_element_type=F32,
+        )
+        run = jnp.zeros((heads, 1), F32)
+        for i in range(tiles):
+            part = inside[i * heads : (i + 1) * heads] + run
+            d_ref[:, i * tile : (i + 1) * tile] = part
+            run = part[:, tile - 1 :]
+
     tot[me] = jnp.broadcast_to(run, tot.shape[1:])
-    pl.semaphore_wait(barrier, toks - 1 + heads_ax - 1)
+    with jax.named_scope("barrier"):
+        pl.semaphore_wait(barrier, toks - 1 + heads_ax - 1)
 
     def tot_copy(peer, slot):
         return pltpu.make_async_remote_copy(
@@ -94,21 +110,28 @@
             device_id={"tok": peer}, device_id_type=MESH,
         )
 
-    vt[...] = x_ref[...].T
-    kt[...] = k_ref[...].T.astype(F32)
-    to_end = jnp.exp(run - d_ref[...])
-    for c in range(chunks):
-        for h in range(c * per, (c + 1) * per):
-            scaled = (kt[...] * to_end[h : h + 1]).astype(BF16)
-            state[h * size : (h + 1) * size] = dot_t(vt[h * size : (h + 1) * size], scaled)
-        state_copy(state, 0, c, partner).start()
-
-    gt[...] = gate_ref[...].T
-    qt = q_ref[...].T
-    depth = qt.shape[0]
-    qq[:depth] = qt
-    qq[depth:] = qt
-    score[...] = dot_t(k_ref[...], q_ref[...])
+    with jax.named_scope("states"):
+        loads["k"].wait()
+        loads["x"].wait()
+        vt[...] = x_ref[...].T
+        kt[...] = k_ref[...].T.astype(F32)
+        to_end = jnp.exp(run - d_ref[...])
+        for c in range(chunks):
+            for h in range(c * per, (c + 1) * per):
+                scaled = (kt[...] * to_end[h : h + 1]).astype(BF16)
+                state[h * size : (h + 1) * size] = dot_t(vt[h * size : (h + 1) * size], scaled)
+            state_copy(state, 0, c, partner).start()
+
+    with jax.named_scope("scores"):
+        loads["gate"].wait()
+        gt[...] = gate_ref[...].T
+        loads["q"].wait()
+        loads["w"].wait()
+        qt = q_ref[...].T
+        depth = qt.shape[0]
+        qq[:depth] = qt
+        qq[depth:] = qt
+        score[...] = dot_t(k_ref[...], q_ref[...])
 
     groups = tile // 8
     t_at = lax.broadcasted_iota(jnp.int32, (groups, tile), 1)
@@ -235,7 +258,8 @@
 
     for k in range(chunks + tree - 1):
         if k < chunks:
-            lax.fori_loop(k * per, (k + 1) * per, near, 0)
+            with jax.named_scope("near"):
+                lax.fori_loop(k * per, (k + 1) * per, near, 0)
         if k == 0:
             for i in range(1, toks):
                 tot_copy(me, lax.rem(me + i, toks)).wait_recv()
@@ -252,15 +276,19 @@
                 fac_all[b] = jnp.exp(full)
         for b in range(tree):
             if 0 <= k - b < chunks:
-                comm(b, k - b)
+                with jax.named_scope(f"exchange_{b}"):
+                    comm(b, k - b)
         for b in range(tree):
             if 0 <= k - b < chunks:
-                distant(b, k - b)
-
-    total = jnp.zeros((1, block), F32)
-    for h in range(heads):
-        g = base[h * size : (h + 1) * size]
-        total = total + jnp.sum(g * g, axis=0, keepdims=True)
+                with jax.named_scope(f"distant_{b}"):
+                    distant(b, k - b)
+
+    with jax.named_scope("squares"):
+        total = jnp.zeros((1, block), F32)
+        for h in range(heads):
+            g = base[h * size : (h + 1) * size]
+            total = total + jnp.sum(g * g, axis=0, keepdims=True)
+
     ssq[my_head] = total
 
     def sq_copy(peer, slot):
@@ -271,19 +299,24 @@
 
     for i in range(1, heads_ax):
         sq_copy(lax.rem(my_head + i, heads_ax), my_head).start()
-    turned[...] = base[...].T * gain_ref[...]
-    for i in range(1, heads_ax):
-        sq_copy(my_head, lax.rem(my_head + i, heads_ax)).wait_recv()
-    squares = ssq[0]
-    for m in range(1, heads_ax):
-        squares = squares + ssq[m]
-    scaling = lax.rsqrt(squares / (width * heads_ax) + epsilon)
-    for i in range(tiles):
-        s = slice(i * tile, (i + 1) * tile)
-        by = column(scaling[:, s], tile)
-        for j in range(width // tile):
-            c = slice(j * tile, (j + 1) * tile)
-            out_ref[s, c] = (turned[s, c] * by).astype(BF16)
+    with jax.named_scope("turn"):
+        turned[...] = base[...].T * gain_ref[...]
+
+    with jax.named_scope("wait_squares"):
+        for i in range(1, heads_ax):
+            sq_copy(my_head, lax.rem(my_head + i, heads_ax)).wait_recv()
+
+    with jax.named_scope("scale"):
+        squares = ssq[0]
+        for m in range(1, heads_ax):
+            squares = squares + ssq[m]
+        scaling = lax.rsqrt(squares / (width * heads_ax) + epsilon)
+        for i in range(tiles):
+            s = slice(i * tile, (i + 1) * tile)
+            by = column(scaling[:, s], tile)
+            for j in range(width // tile):
+                c = slice(j * tile, (j + 1) * tile)
+                out_ref[s, c] = (turned[s, c] * by).astype(BF16)
 
     for i in range(1, toks):
         tot_copy(lax.rem(me + i, toks), me).wait_send()
@@ -307,12 +340,21 @@
     tile = 128
     chunks = min(4, heads)
     vmem = pl.BlockSpec(memory_space=pltpu.VMEM)
+    hbm = pl.BlockSpec(memory_space=pltpu.HBM)
+    weight = w.transpose(2, 1, 0)
     return pl.pallas_call(
         functools.partial(kernel, (toks, heads_ax, tile, chunks)),
         out_shape=jax.ShapeDtypeStruct((block, width), BF16),
-        in_specs=[vmem] * 5 + [pl.BlockSpec(memory_space=pltpu.SMEM)] + [vmem] * 2,
+        in_specs=[hbm] * 5 + [pl.BlockSpec(memory_space=pltpu.SMEM), hbm, vmem],
         out_specs=vmem,
         scratch_shapes=[
+            pltpu.VMEM(x.shape, BF16),
+            pltpu.VMEM(k.shape, BF16),
+            pltpu.VMEM(q.shape, BF16),
+            pltpu.VMEM((heads, block), F32),
+            pltpu.VMEM(weight.shape, F32),
+            pltpu.VMEM(gate.shape, BF16),
+            pltpu.SemaphoreType.DMA((6,)),
             pltpu.VMEM((heads, block), F32),
             pltpu.VMEM((toks, heads, depth), F32),
             pltpu.VMEM((tree, heads, depth), F32),
@@ -337,9 +379,9 @@
             pltpu.SemaphoreType.DMA((heads_ax,)),
         ],
         compiler_params=pltpu.CompilerParams(
-            collective_id=0, has_side_effects=True, vmem_limit_bytes=40 * 2**20
+            collective_id=0, has_side_effects=True, vmem_limit_bytes=60 * 2**20
         ),
-    )(x, k, q, ld.T, w.transpose(2, 1, 0), skip, gate, gain[None, :])
+    )(x, k, q, ld.T, weight, skip, gate, gain[None, :])
 
 
 def solution(mesh):

time: 33.2 us -> 28.9 us (0.87)
  local copies, waits for them, and re-layouts: 7.05 us -> 1.87 us
  Pallas kernels: 25.8 us -> 26.8 us
    unnamed x17 -> x1, local copies, waits for them, and re-layouts: 7.05 us -> 1.87 us
    pallas_call x1, Pallas kernels: 25.8 us -> 26.8 us  [shards(): pl.pallas_call(functools.partial(kernel, (toks, heads_ax, tile, chunks)),...]
where the time goes in v2:
time: 28.9 us; the launch traced here: 28.7 us
  Pallas kernels  26.8 us (93%)
  local copies, waits for them, and re-layouts  1.87 us (6%)
    pallas_call x1, Pallas kernels, shards(): pl.pallas_call(functools.partial(kernel, (toks, heads_ax, tile, chunks)),...  26.8 us
    unnamed x1, local copies, waits for them, and re-layouts  1.87 us

profile of v2, /device:TPU:27, one launch (start us, length us, event | category | flops | bytes accessed | tf_op | source)
XLA Modules:
  0.0 28.7 jit_solution(13902472914593126190)
XLA Ops:
  0.0 26.8 %shard_map.82 = bf16[512,512]{1,0:T(8,128)(2,1)} custom-call(bf16[512,512]{1,0:T(8,128)(2,1)} %x_in.1, bf16[512,128]{1,0:T(8,128)(2,1)} %k_in.1, bf16[512,128]{1,0:T(8,128)(2,1)} %q_in.1, f32[8,512]{1,0:T(8,128)} %bitcast.4, f32[18,8,512]{2,1,0:T(8,128)} %bitcast.3, f32[8]{0:T(128)} %skip_ref.1, bf16[512,512]{1,0:T(8,128)(2,1)} %gate_in.1, f32[1,512]{1,0:T(1,128)} %bitcast.5), custom_call_target="tpu_custom_call" | custom-call | tf_op jit(solution)/shard_map/pallas_call | solution.py:345
  26.8 1.9 %copy.10 = bf16[512,512]{1,0:T(8,128)(2,1)} copy(bf16[512,512]{1,0:T(8,128)(2,1)} %shard_map.82) | data formatting | bytes 1048576
